TPU v7x, 256 devices: a whole 4x4x8 slice. The times are simulated.
256 devices in a mesh: blk: 8 (over y, x_hi), group: 32 (over z, x_lo, core).
Axes of the slice: x: 4 (x_hi: 2, x_lo: 2; x = x_hi * 2 + x_lo), y: 4, z: 8, core: 2. Of those that a mesh axis runs over, the one named last changes fastest.
Arguments:
- img_emb: bfloat16 [16384, 1152], P(('blk', 'group')), may hold values from -6 to 6
- txt_emb: bfloat16 [16384, 1152], P(('blk', 'group')), may hold values from -6 to 6
- img_ids: int32 [16384], P(('blk', 'group')), may hold values from 0 to 1023
- txt_ids: int32 [16384], P(('blk', 'group')), may hold values from 0 to 1023
- scale_logarithm: float32 [1], replicated, may hold values from 3.7 to 4.4
- bias: float32 [1], replicated, may hold values from -4 to -2
Outputs:
- img_grad: float32 [16384, 1152], P(('blk', 'group'))
- txt_grad: float32 [16384, 1152], P(('blk', 'group'))
All inputs are finite; a program needn't handle non-finite values.
Results may differ from a plain program's by a relative error of at most 0.0093.
Values may be sent and summed in bfloat16 or wider, within the bound.
A program may use at most 64 MiB of HBM per device.

v0:
```python
import functools

import jax
import jax.numpy as jnp
from jax import lax
from jax.experimental import pallas as pl
from jax.experimental.pallas import tpu as pltpu
from jax.sharding import PartitionSpec as P

MESH = pl.DeviceIdType.MESH
D = 1152
OWN = 64
HALF = 32
QUART = 16
ROWS = 1024
N_COPIES = 160

IMG_ORDER = [
    (4, 1), (4, 0),
    (3, 1), (5, 1), (3, 0), (5, 0),
    (2, 1), (6, 1), (2, 0), (6, 0),
    (1, 1), (7, 1), (0, 1), (1, 0), (7, 0), (0, 0),
]
IMG_ROW = {key: OWN * place for place, key in enumerate(IMG_ORDER)}

TXT_BASE = {
    ("A", 2): 0, ("B", 2): 128,
    ("A", 1): 256, ("A", 3): 384, ("B", 1): 512, ("B", 3): 640,
    ("A", 0): 768, ("B", 0): 896,
}


def txt_row(path, second, first):
    return TXT_BASE[path, second] + HALF * first


def unit_rows(embedding):
    widened = embedding.astype(jnp.float32)
    inverse = lax.rsqrt(jnp.sum(widened * widened, axis=1, keepdims=True) + 1e-06)
    return widened * inverse, inverse


def kernel(
    img_ref, txt_ref, ids_ref, scale_ref, bias_ref, img_out, txt_out,
    imgs, txts, img_tiles, txt_tiles, img_col, txt_line, coef, coef_t, img_part, txt_part,
    t1_send, t1_recv, t2_send, t2_recv, t3_send, t3_recv, t4_send, t4_recv,
    core_send, core_recv, z_send, z_recv, send_sems, recv_sems,
):
    f32, bf16 = jnp.float32, jnp.bfloat16
    blk, grp = lax.axis_index("blk"), lax.axis_index("group")
    y, x_hi = lax.div(blk, 2), lax.rem(blk, 2)
    z, x_lo, core = lax.div(grp, 4), lax.rem(lax.div(grp, 2), 2), lax.rem(grp, 2)
    x = x_hi * 2 + x_lo

    def device(dx=0, dy=0, dz=0, dc=0):
        nx, ny, nz = lax.rem(x + dx + 4, 4), lax.rem(y + dy + 4, 4), lax.rem(z + dz + 8, 8)
        nc = lax.rem(core + dc, 2)
        return (ny * 2 + lax.div(nx, 2), (nz * 2 + lax.rem(nx, 2)) * 2 + nc)

    near = {
        "x+": device(dx=1), "x-": device(dx=-1), "x2": device(dx=2),
        "y+": device(dy=1), "y-": device(dy=-1), "y2": device(dy=2),
        "z+": device(dz=1), "z-": device(dz=-1), "z+2": device(dz=2), "z-2": device(dz=-2), "z4": device(dz=4),
        "core": device(dc=1),
    }
    started = []

    def send(src, dst, to):
        number = len(started)
        copy = pltpu.make_async_remote_copy(
            src_ref=src, dst_ref=dst, send_sem=send_sems.at[number], recv_sem=recv_sems.at[number],
            device_id=near[to], device_id_type=MESH,
        )
        copy.start()
        started.append(copy)
        return copy

    barrier = pltpu.get_barrier_semaphore()
    for there in near.values():
        pl.semaphore_signal(barrier, inc=1, device_id=there, device_id_type=MESH)

    own_img, own_txt = IMG_ROW[0, 0], {p: txt_row(p, 0, 0) for p in "AB"}
    imgs[own_img:own_img + OWN, :] = unit_rows(img_ref[...])[0].astype(bf16)
    unit = unit_rows(txt_ref[...])[0].astype(bf16)
    txts[own_txt["A"]:own_txt["A"] + HALF, :] = unit[:HALF]
    txts[own_txt["B"]:own_txt["B"] + HALF, :] = unit[HALF:]
    img_tiles[0, 0] = ids_ref[0]
    txt_tiles[0, 0] = ids_ref[1]
    pl.semaphore_wait(barrier, len(near))

    first_axis, second_axis = {"A": "x", "B": "y"}, {"A": "y", "B": "x"}

    def text(path, second, first, low=0, high=HALF):
        row = txt_row(path, second, first)
        return txts.at[row + low:row + high, :]

    def image(dz, cr, low=0, high=OWN):
        row = IMG_ROW[dz, cr]
        return imgs.at[row + low:row + high, :]

    def send_text(path, src, dst, axis, way, low=0, high=HALF):
        return send(text(path, *src, low, high), text(path, *dst, low, high), axis[path] + way)

    def send_image(src, dst, way, low, high):
        return send(image(src, 0, low, high), image(dst, 0, low, high), "z" + way)

    hop = {}
    hop["idc"] = send(img_tiles.at[0, 0], img_tiles.at[0, 1], "core")
    hop["idx1"] = send(txt_tiles.at[0, 0], txt_tiles.at[0, 1], "x+")
    for p in "AB":
        hop[p, 0, 1] = send_text(p, (0, 0), (0, 1), first_axis, "+")
        hop[p, 0, 3] = send_text(p, (0, 0), (0, 3), first_axis, "-")
    for half in (0, 1):
        hop["z", 1, half] = send_image(0, 1, "+", HALF * half, HALF * half + HALF)
        hop["z", 7, half] = send_image(0, 7, "-", HALF * half, HALF * half + HALF)
    for p in "AB":
        hop[p, 1, 0] = send_text(p, (0, 0), (1, 0), second_axis, "+")
        hop[p, 3, 0] = send_text(p, (0, 0), (3, 0), second_axis, "-")
    hop["c", 0] = send(image(0, 0), image(0, 1), "core")
    hop["idc"].wait_recv()
    hop["idz1"] = send(img_tiles.at[0], img_tiles.at[1], "z+")
    hop["idx1"].wait_recv()
    hop["idx2"] = send(txt_tiles.at[0, 0:2], txt_tiles.at[0, 2:4], "x2")

    for p in "AB":
        hop[p, 0, 1].wait_recv()
        hop[p, 0, 3].wait_recv()
        hop[p, 0, 2, 0] = send_text(p, (0, 1), (0, 2), first_axis, "+", 0, QUART)
        hop[p, 0, 2, 1] = send_text(p, (0, 3), (0, 2), first_axis, "-", QUART, HALF)
        for e in (1, 3):
            hop[p, 1, e] = send_text(p, (0, e), (1, e), second_axis, "+")
            hop[p, 3, e] = send_text(p, (0, e), (3, e), second_axis, "-")

    def pass_images(k):
        for half in (0, 1):
            hop["z", k, half].wait_recv()
            if k < 3 or half == 0:
                hop["z", k + 1, half] = send_image(k, k + 1, "+", HALF * half, HALF * half + HALF)
            hop["z", 8 - k, half].wait_recv()
            if k < 3 or half == 1:
                hop["z", 7 - k, half] = send_image(8 - k, 7 - k, "-", HALF * half, HALF * half + HALF)
        for dz in (k, 8 - k):
            hop["c", dz] = send(image(dz, 0), image(dz, 1), "core")

    pass_images(1)
    hop["idz1"].wait_recv()
    hop["idz2"] = send(img_tiles.at[0:2], img_tiles.at[2:4], "z+2")
    hop["idx2"].wait_recv()
    hop["idy1"] = send(txt_tiles.at[0], txt_tiles.at[1], "y+")
    for p in "AB":
        hop[p, 1, 0].wait_recv()
        hop[p, 2, 0] = send_text(p, (1, 0), (2, 0), second_axis, "+")
        hop[p, 3, 0].wait_recv()
        hop[p, 0, 2, 0].wait_recv()
        hop[p, 0, 2, 1].wait_recv()
        hop[p, 1, 2] = send_text(p, (0, 2), (1, 2), second_axis, "+")
        hop[p, 3, 2] = send_text(p, (0, 2), (3, 2), second_axis, "-")
    for p in "AB":
        hop[p, 1, 1].wait_recv()
        hop[p, 2, 1] = send_text(p, (1, 1), (2, 1), second_axis, "+")
        hop[p, 3, 3].wait_recv()
        hop[p, 2, 3] = send_text(p, (3, 3), (2, 3), second_axis, "-")
    pass_images(2)
    hop["idz2"].wait_recv()
    hop["idz4"] = send(img_tiles.at[0:4], img_tiles.at[4:8], "z4")
    hop["idy1"].wait_recv()
    hop["idy2"] = send(txt_tiles.at[0:2], txt_tiles.at[2:4], "y2")
    for p in "AB":
        hop[p, 1, 3].wait_recv()
        hop[p, 3, 1].wait_recv()
        hop[p, 1, 2].wait_recv()
        hop[p, 3, 2].wait_recv()
        hop[p, 2, 2] = send_text(p, (3, 2), (2, 2), second_axis, "-")
    pass_images(3)
    hop["z", 4, 0].wait_recv()
    hop["z", 4, 1].wait_recv()
    hop["c", 4] = send(image(4, 0), image(4, 1), "core")

    hop["idz4"].wait_recv()
    hop["idy2"].wait_recv()
    lane = lax.broadcasted_iota(jnp.int32, (1, 128), 1)
    for (p, d), base in TXT_BASE.items():
        row = 0 if p == "A" else 1
        line = None
        for e in range(4):
            tile = (txt_tiles[d, e] if p == "A" else txt_tiles[e, d])[row:row + 1, :]
            line = tile if line is None else jnp.where(lane < HALF * e, line, tile)
        txt_line[:, base:base + 128] = line
    for place in range(0, 16, 2):
        (z0, c0), (z1, c1) = IMG_ORDER[place], IMG_ORDER[place + 1]
        line = jnp.where(lane < OWN, img_tiles[z0, c0][0:1, :], img_tiles[z1, c1][0:1, :])
        img_col[OWN * place:OWN * place + 128, :] = jnp.transpose(jnp.broadcast_to(line, (128, 128)))

    for p in "AB":
        for e in range(4):
            hop[p, 2, e].wait_recv()
    for dz in range(8):
        hop["c", dz].wait_recv()

    scale = jnp.exp(jnp.full((1, 256), scale_ref[0], f32))
    half_scale, half_bias = 0.5 * scale, jnp.full((1, 256), 0.5 * bias_ref[0], f32)

    def score_tile(step, carry):
        r = pl.multiple_of(lax.div(step, 4) * 256, 256)
        t = pl.multiple_of(lax.rem(step, 4) * 256, 256)
        scores = lax.dot_general(
            imgs[pl.ds(r, 256), :], txts[pl.ds(t, 256), :], (((1,), (1,)), ((), ())), preferred_element_type=f32
        )
        column = img_col[pl.ds(r, 256), :]
        same = jnp.concatenate([column, column], axis=1) == txt_line[:, pl.ds(t, 256)]
        value = 0.5 * jnp.tanh(half_scale * scores + half_bias) + jnp.where(same, -0.5, 0.5)
        coef[pl.ds(r, 256), pl.ds(t, 256)] = value.astype(bf16)
        coef_t[pl.ds(t, 256), pl.ds(r, 256)] = jnp.transpose(value).astype(bf16)
        return carry

    lax.fori_loop(0, 16, score_tile, 0)

    def img_terms(row, count):
        img_part[row:row + count, :] = jnp.dot(coef[row:row + count, :], txts[...], preferred_element_type=f32)

    def txt_terms(row, count):
        txt_part[row:row + count, :] = jnp.dot(coef_t[row:row + count, :], imgs[...], preferred_element_type=f32)

    def to_core(dz):
        row = IMG_ROW[dz, 1]
        core_send[OWN * dz:OWN * dz + OWN, :] = img_part[row:row + OWN, :].astype(bf16)
        hop["s", dz] = send(core_send.at[OWN * dz:OWN * dz + OWN], core_recv.at[OWN * dz:OWN * dz + OWN], "core")

    def chip_sum(dz, low=0, high=OWN):
        row = IMG_ROW[dz, 0]
        return img_part[row + low:row + high, :] + core_recv[OWN * dz + low:OWN * dz + high, :].astype(f32)

    def z_out(dz, low, high, total, way):
        rows = slice(OWN * dz + low, OWN * dz + high)
        z_send[rows, :] = total.astype(bf16)
        return send(z_send.at[rows], z_recv.at[rows], "z" + way)

    def z_step(k):
        down, up = 4 - k, 4 + k
        if k == 0:
            hop["s", 4].wait_recv()
            hop["r", 4, 0] = z_out(4, 0, HALF, chip_sum(4, 0, HALF), "-")
            hop["r", 4, 1] = z_out(4, HALF, OWN, chip_sum(4, HALF, OWN), "+")
            return
        hop["s", down].wait_recv()
        hop["s", up].wait_recv()
        for half in (0, 1):
            low, high = HALF * half, HALF * half + HALF
            for dz, before, way, lone in ((down, down + 1, "-", 1), (up, up - 1, "+", 0)):
                total = chip_sum(dz, low, high)
                if k > 1 or half != lone:
                    hop["r", before, half].wait_recv()
                    total = total + z_recv[OWN * before + low:OWN * before + high, :].astype(f32)
                hop["r", dz, half] = z_out(dz, low, high, total, way)

    def txt_far():
        for p in "AB":
            base, at = TXT_BASE[p, 2], 128 * "AB".index(p)
            t1_send[at:at + 128, :] = txt_part[base:base + 128, :].astype(bf16)
            for part, way in ((0, "-"), (1, "+")):
                rows = slice(at + OWN * part, at + OWN * part + OWN)
                hop["t1", p, part] = send(t1_send.at[rows], t1_recv.at[rows], second_axis[p] + way)

    def txt_near():
        for p in "AB":
            for part, d, way in ((0, 1, "-"), (1, 3, "+")):
                base, at = TXT_BASE[p, d], 256 * "AB".index(p) + 128 * part
                got = 128 * "AB".index(p) + OWN * part
                hop["t1", p, part].wait_recv()
                add, keep = OWN * part, OWN * (1 - part)
                t2_send[at + add:at + add + OWN, :] = (
                    txt_part[base + add:base + add + OWN, :] + t1_recv[got:got + OWN, :].astype(f32)
                ).astype(bf16)
                t2_send[at + keep:at + keep + OWN, :] = txt_part[base + keep:base + keep + OWN, :].astype(bf16)
                hop["t2", p, part] = send(
                    t2_send.at[at:at + 128], t2_recv.at[at:at + 128], second_axis[p] + way
                )

    def txt_line_sum(p, first):
        base, at = TXT_BASE[p, 0] + HALF * first, 256 * "AB".index(p) + HALF * first
        return (
            txt_part[base:base + HALF, :]
            + t2_recv[at:at + HALF, :].astype(f32)
            + t2_recv[at + 128:at + 128 + HALF, :].astype(f32)
        )

    def txt_far_first(p):
        for part in (0, 1):
            hop["t2", p, part].wait_recv()
        at = HALF * "AB".index(p)
        t3_send[at:at + HALF, :] = txt_line_sum(p, 2).astype(bf16)
        for part, way in ((0, "-"), (1, "+")):
            rows = slice(at + QUART * part, at + QUART * part + QUART)
            hop["t3", p, part] = send(t3_send.at[rows], t3_recv.at[rows], first_axis[p] + way)

    def txt_near_first(p):
        for part, first, way in ((0, 1, "-"), (1, 3, "+")):
            total = txt_line_sum(p, first)
            hop["t3", p, part].wait_recv()
            got = t3_recv[HALF * "AB".index(p) + QUART * part:HALF * "AB".index(p) + QUART * part + QUART, :].astype(f32)
            at = OWN * "AB".index(p) + HALF * part
            if part == 0:
                t4_send[at:at + QUART, :] = (total[:QUART] + got).astype(bf16)
                t4_send[at + QUART:at + HALF, :] = total[QUART:].astype(bf16)
            else:
                t4_send[at:at + QUART, :] = total[:QUART].astype(bf16)
                t4_send[at + QUART:at + HALF, :] = (total[QUART:] + got).astype(bf16)
            hop["t4", p, part] = send(t4_send.at[at:at + HALF], t4_recv.at[at:at + HALF], first_axis[p] + way)

    def finish(embedding, total):
        unit, inverse = unit_rows(embedding)
        direction = scale[:, 0:1] * total
        return inverse * (direction - unit * jnp.sum(unit * direction, axis=1, keepdims=True))

    txt_terms(0, 256)
    txt_far()
    img_terms(0, 128)
    to_core(4)
    img_terms(128, 256)
    to_core(3)
    to_core(5)
    z_step(0)
    txt_terms(256, 512)
    txt_near()
    img_terms(384, 256)
    to_core(2)
    to_core(6)
    z_step(1)
    img_terms(640, 384)
    to_core(1)
    to_core(7)
    to_core(0)
    z_step(2)
    txt_terms(768, 256)
    txt_far_first("A")
    txt_far_first("B")
    z_step(3)
    txt_near_first("A")
    txt_near_first("B")
    for p in "AB":
        low = HALF * "AB".index(p)
        total = txt_line_sum(p, 0)
        for part in (0, 1):
            hop["t4", p, part].wait_recv()
            at = OWN * "AB".index(p) + HALF * part
            total = total + t4_recv[at:at + HALF, :].astype(f32)
        txt_out[low:low + HALF, :] = finish(txt_ref[low:low + HALF, :], total)
    hop["s", 0].wait_recv()
    for half in (0, 1):
        low, high = HALF * half, HALF * half + HALF
        total = chip_sum(0, low, high)
        for dz in (1, 7):
            hop["r", dz, half].wait_recv()
            total = total + z_recv[OWN * dz + low:OWN * dz + high, :].astype(f32)
        img_out[low:high, :] = finish(img_ref[low:high, :], total)
    for copy in started:
        copy.wait_send()


def body(img_emb, txt_emb, img_ids, txt_ids, scale_logarithm, bias):
    line = jnp.stack([
        jnp.stack([jnp.tile(img_ids, 2)] * 8),
        jnp.stack([jnp.tile(txt_ids[:HALF], 4), jnp.tile(txt_ids[HALF:], 4)] * 4),
    ])
    f32, bf16, i32 = jnp.float32, jnp.bfloat16, jnp.int32
    vmem, smem = pl.BlockSpec(memory_space=pltpu.VMEM), pl.BlockSpec(memory_space=pltpu.SMEM)
    return pl.pallas_call(
        kernel,
        out_shape=(jax.ShapeDtypeStruct((OWN, D), f32), jax.ShapeDtypeStruct((OWN, D), f32)),
        in_specs=[vmem, vmem, vmem, smem, smem],
        out_specs=(vmem, vmem),
        scratch_shapes=[
            pltpu.VMEM((ROWS, D), bf16),
            pltpu.VMEM((ROWS, D), bf16),
            pltpu.VMEM((8, 2, 8, 128), i32),
            pltpu.VMEM((4, 4, 8, 128), i32),
            pltpu.VMEM((ROWS, 128), i32),
            pltpu.VMEM((1, ROWS), i32),
            pltpu.VMEM((ROWS, ROWS), bf16),
            pltpu.VMEM((ROWS, ROWS), bf16),
            pltpu.VMEM((ROWS, D), f32),
            pltpu.VMEM((ROWS, D), f32),
            pltpu.VMEM((256, D), bf16),
            pltpu.VMEM((256, D), bf16),
            pltpu.VMEM((512, D), bf16),
            pltpu.VMEM((512, D), bf16),
            pltpu.VMEM((64, D), bf16),
            pltpu.VMEM((64, D), bf16),
            pltpu.VMEM((128, D), bf16),
            pltpu.VMEM((128, D), bf16),
            pltpu.VMEM((512, D), bf16),
            pltpu.VMEM((512, D), bf16),
            pltpu.VMEM((512, D), bf16),
            pltpu.VMEM((512, D), bf16),
            pltpu.SemaphoreType.DMA((N_COPIES,)),
            pltpu.SemaphoreType.DMA((N_COPIES,)),
        ],
        compiler_params=pltpu.CompilerParams(
            collective_id=0, has_side_effects=True, vmem_limit_bytes=56 * 1024 * 1024
        ),
        cost_estimate=pl.CostEstimate(flops=7247757312, bytes_accessed=900000, transcendentals=1048576),
    )(img_emb, txt_emb, line, scale_logarithm, bias)


def solution(mesh):
    split = P(("blk", "group"), None)
    ids = P(("blk", "group"))
    return jax.shard_map(
        body,
        mesh=mesh,
        in_specs=(split, split, ids, ids, P(), P()),
        out_specs=(split, split),
        check_vma=False,
    )
```

profile of v0, /device:TPU:1, one launch (start us, length us, event | category | flops | bytes accessed | tf_op | source)
XLA Modules:
  0.0 71.2 jit_solution(15672758365085332409)
XLA Ops:
  1.3 0.0 copy-start.2
  1.9 0.0 copy-done.2
  2.0 0.0 copy-start.1
  2.0 0.1 stack_tile.6
  2.1 0.6 copy-done.1
  2.6 0.1 fusion
  2.7 0.1 stack_tile.8
  2.8 0.1 stack_tile.7
  2.9 0.6 pad_add_fusion.ids_ref
  3.5 65.2 %shard_map.77 = (f32[64,1152]{1,0:T(8,128)}, f32[64,1152]{1,0:T(8,128)}) custom-call(bf16[64,1152]{1,0:T(8,128)(2,1)} %img_ref.1, bf16[64,1152]{1,0:T(8,128)(2,1)} %txt_ref.1, s32[2,8,128]{2,1,0:T(8,128)} %pad_add_fusion.ids_ref, f32[1]{0:T(128)S(6)} %copy.10.scale_ref, f32[1]{0:T(128)S(6)} %copy.11.bias_ref), custom_call_target="tpu_custom_call" | custom-call | flops 7247757312 | bytes 900000 | tf_op jit(solution)/shard_map/pallas_call | solution.py:367
  68.8 0.0 copy-start
  68.8 1.7 %copy.12 = f32[64,1152]{1,0:T(8,128)} copy(f32[64,1152]{1,0:T(8,128)} %get-tuple-element.6) | data formatting | bytes 589824
  70.5 0.0 copy-done
  70.5 0.7 %copy.13 = f32[64,1152]{1,0:T(8,128)} copy(f32[64,1152]{1,0:T(8,128)S(1)} %copy-done) | data formatting | bytes 589824
  (5 shorter events, 0.0 us)
Async XLA Ops:
  1.3 0.7 copy-start.2
  2.0 0.7 copy-start.1
  68.8 1.8 %copy-start = (f32[64,1152]{1,0:T(8,128)S(1)}, f32[64,1152]{1,0:T(8,128)}, u32[]{:S(2)}) copy-start(f32[64,1152]{1,0:T(8,128)} %get-tuple-element.7) | copy-start | bytes 884740
where the time goes:
time: 71.4 us; the launch traced here: 71.2 us
  Pallas kernels  65.2 us (91%)
  local copies, waits for them, and re-layouts  3.39 us (5%)
  between operations  2 us (3%)
    pallas_call x1, Pallas kernels, body(): pl.pallas_call(kernel, out_shape=(jax.ShapeDtypeStruct((OWN, D), f32), ja...  65.2 us
    unnamed x8, local copies, waits for them, and re-layouts  3.03 us

commit v1 on v0

v1 whole, which is shorter than its diff:
```python
import functools

import jax
import jax.numpy as jnp
from jax import lax
from jax.experimental import pallas as pl
from jax.experimental.pallas import tpu as pltpu
from jax.sharding import PartitionSpec as P

MESH = pl.DeviceIdType.MESH
D = 1152
OWN = 64
HALF = 32
QUART = 16
ROWS = 1024
N_COPIES = 224
PIECE = 32

IMG_ORDER = [
    (4, 1), (4, 0),
    (3, 1), (5, 1), (3, 0), (5, 0),
    (2, 1), (6, 1), (2, 0), (6, 0),
    (1, 1), (7, 1), (0, 1), (1, 0), (7, 0), (0, 0),
]
IMG_ROW = {key: OWN * place for place, key in enumerate(IMG_ORDER)}

TXT_BASE = {
    ("A", 2): 0, ("B", 2): 128,
    ("A", 1): 256, ("A", 3): 384, ("B", 1): 512, ("B", 3): 640,
    ("A", 0): 768, ("B", 0): 896,
}


def txt_row(path, second, first):
    return TXT_BASE[path, second] + HALF * first


def unit_rows(embedding):
    widened = embedding.astype(jnp.float32)
    inverse = lax.rsqrt(jnp.sum(widened * widened, axis=1, keepdims=True) + 1e-06)
    return widened * inverse, inverse


def kernel(
    img_ref, txt_ref, img_ids_ref, txt_ids_ref, scale_ref, bias_ref, img_out, txt_out,
    imgs, txts, img_ids, txt_ids, img_col, txt_line, coef, img_part, txt_part,
    t1_send, t1_recv, t2_send, t2_recv, t3_send, t3_recv, t4_send, t4_recv,
    core_send, core_recv, z_send, z_recv, send_sems, recv_sems,
):
    f32, bf16 = jnp.float32, jnp.bfloat16
    blk, grp = lax.axis_index("blk"), lax.axis_index("group")
    y, x_hi = lax.div(blk, 2), lax.rem(blk, 2)
    z, x_lo, core = lax.div(grp, 4), lax.rem(lax.div(grp, 2), 2), lax.rem(grp, 2)
    x = x_hi * 2 + x_lo

    def device(dx=0, dy=0, dz=0, dc=0):
        nx, ny, nz = lax.rem(x + dx + 4, 4), lax.rem(y + dy + 4, 4), lax.rem(z + dz + 8, 8)
        nc = lax.rem(core + dc, 2)
        return (ny * 2 + lax.div(nx, 2), (nz * 2 + lax.rem(nx, 2)) * 2 + nc)

    near = {
        "x+": device(dx=1), "x-": device(dx=-1), "y+": device(dy=1), "y-": device(dy=-1),
        "z+": device(dz=1), "z-": device(dz=-1), "core": device(dc=1),
    }
    started = []
    hop = {}

    def send(key, src, dst, to):
        number = len(started)
        copy = pltpu.make_async_remote_copy(
            src_ref=src, dst_ref=dst, send_sem=send_sems.at[number], recv_sem=recv_sems.at[number],
            device_id=near[to], device_id_type=MESH,
        )
        copy.start()
        started.append(copy)
        hop[key] = copy

    barrier = pltpu.get_barrier_semaphore()
    for there in near.values():
        pl.semaphore_signal(barrier, inc=1, device_id=there, device_id_type=MESH)

    own_img, own_txt = IMG_ROW[0, 0], {p: txt_row(p, 0, 0) for p in "AB"}
    imgs[own_img:own_img + OWN, :] = unit_rows(img_ref[...])[0].astype(bf16)
    unit = unit_rows(txt_ref[...])[0].astype(bf16)
    txts[own_txt["A"]:own_txt["A"] + HALF, :] = unit[:HALF]
    txts[own_txt["B"]:own_txt["B"] + HALF, :] = unit[HALF:]
    line = img_ids_ref[...]
    img_ids[own_img // OWN] = jnp.concatenate([line] * 2, axis=1)
    line = txt_ids_ref[...]
    txt_ids[own_txt["A"] // HALF] = jnp.concatenate([line[:, :HALF]] * 4, axis=1)
    txt_ids[own_txt["B"] // HALF] = jnp.concatenate([line[:, HALF:]] * 4, axis=1)
    pl.semaphore_wait(barrier, len(near))

    first_axis, second_axis = {"A": "x", "B": "y"}, {"A": "y", "B": "x"}

    def text(path, second, first, low=0, high=HALF):
        row = txt_row(path, second, first)
        return txts.at[row + low:row + high, :]

    def text_id(path, second, first):
        return txt_ids.at[txt_row(path, second, first) // HALF]

    def image(dz, cr, low=0, high=OWN):
        row = IMG_ROW[dz, cr]
        return imgs.at[row + low:row + high, :]

    def image_id(dz, cr):
        return img_ids.at[IMG_ROW[dz, cr] // OWN]

    pieces = [(low, low + PIECE) for low in range(0, OWN, PIECE)]

    def send_text(p, src, dst, axis, way):
        send((p, *dst), text(p, *src), text(p, *dst), axis[p] + way)
        send((p, *dst, "id"), text_id(p, *src), text_id(p, *dst), axis[p] + way)

    def got_text(p, *slot):
        hop[(p, *slot)].wait_recv()
        hop[(p, *slot, "id")].wait_recv()

    def both_ways(e):
        for p in "AB":
            for d, way in ((1, "+"), (3, "-")):
                send_text(p, (0, e), (d, e), second_axis, way)

    def image_piece(dz, low, high):
        if dz:
            hop["z", dz, low].wait_recv()
        for src, way, step in ((dz, "+", 1), (dz, "-", -1)):
            dst = (dz + step) % 8
            if dz and (dz < 4) != (step > 0) or dz == 4:
                continue
            if dst == 4 and (low < HALF) != (step > 0):
                continue
            send(("z", dst, low), image(dz, 0, low, high), image(dst, 0, low, high), "z" + way)

    def image_ids(dz):
        if dz:
            hop["z", dz, "id"].wait_recv()
        for way, step in (("+", 1), ("-", -1)):
            dst = (dz + step) % 8
            if dz and (dz < 4) != (step > 0) or dz == 4 or dst == 4 and step < 0:
                continue
            send(("z", dst, "id"), image_id(dz, 0), image_id(dst, 0), "z" + way)

    def across(dz, low, high):
        send(("c", dz, low), image(dz, 0, low, high), image(dz, 1, low, high), "core")

    def across_ids(dz):
        send(("c", dz, "id"), image_id(dz, 0), image_id(dz, 1), "core")

    def pass_images(k, index):
        low, high = pieces[index]
        for dz in (k, 8 - k):
            image_piece(dz, low, high)
        if high == OWN:
            for dz in (k, 8 - k):
                image_ids(dz)
        for dz in (k, 8 - k):
            across(dz, low, high)
            if high == OWN:
                across_ids(dz)

    def got_images(*blocks):
        for dz in blocks:
            for low, _ in pieces:
                hop["c", dz, low].wait_recv()
            hop["c", dz, "id"].wait_recv()

    lane = lax.broadcasted_iota(jnp.int32, (1, 128), 1)

    def lines_of_text(*seconds):
        for d in seconds:
            for p in "AB":
                base, line = TXT_BASE[p, d], None
                for e in range(4):
                    ids = txt_ids[base // HALF + e]
                    line = ids if line is None else jnp.where(lane < HALF * e, line, ids)
                txt_line[:, base:base + 128] = line

    def columns_of_images(low, high):
        for row in range(low, high, 128):
            place = row // OWN
            line = jnp.where(lane < OWN, img_ids[place], img_ids[place + 1])
            img_col[row:row + 128, :] = jnp.transpose(jnp.broadcast_to(line, (128, 128)))

    scale = jnp.exp(jnp.full((1, 256), scale_ref[0], f32))
    half_scale, half_bias = 0.5 * scale, jnp.full((1, 256), 0.5 * bias_ref[0], f32)

    def score_tile(r, rows, t):
        scores = lax.dot_general(
            imgs[r:r + rows, :], txts[t:t + 256, :], (((1,), (1,)), ((), ())), preferred_element_type=f32
        )
        column = img_col[r:r + rows, :]
        same = jnp.concatenate([column, column], axis=1) == txt_line[:, t:t + 256]
        value = 0.5 * jnp.tanh(half_scale * scores + half_bias) + jnp.where(same, -0.5, 0.5)
        coef[r:r + rows, t:t + 256] = value.astype(bf16)

    for p in "AB":
        for e, way in ((1, "+"), (3, "-")):
            send_text(p, (0, 0), (0, e), first_axis, way)
    for low, high in pieces:
        image_piece(0, low, high)
    image_ids(0)
    both_ways(0)
    for low, high in pieces:
        across(0, low, high)
    across_ids(0)

    for p in "AB":
        got_text(p, 0, 1)
        got_text(p, 0, 3)
        send((p, 0, 2), text(p, 0, 1, 0, QUART), text(p, 0, 2, 0, QUART), first_axis[p] + "+")
        send((p, 0, 2, "id"), text_id(p, 0, 1), text_id(p, 0, 2), first_axis[p] + "+")
        send((p, 0, 2, "b"), text(p, 0, 3, QUART, HALF), text(p, 0, 2, QUART, HALF), first_axis[p] + "-")
        for d, way, order in ((1, "+", (1, 3)), (3, "-", (3, 1))):
            for e in order:
                send_text(p, (0, e), (d, e), second_axis, way)
    pass_images(1, 0)
    for p in "AB":
        got_text(p, 1, 0)
        send_text(p, (1, 0), (2, 0), second_axis, "+")
    pass_images(1, 1)
    for p in "AB":
        got_text(p, 3, 0)
        got_text(p, 0, 2)
        hop[p, 0, 2, "b"].wait_recv()
    both_ways(2)
    lines_of_text(0)
    pass_images(2, 0)
    got_images(0, 1, 7)
    columns_of_images(640, 1024)
    score_tile(640, 384, 768)
    for p in "AB":
        got_text(p, 1, 1)
        send_text(p, (1, 1), (2, 1), second_axis, "+")
        got_text(p, 3, 3)
        send_text(p, (3, 3), (2, 3), second_axis, "-")
    pass_images(2, 1)
    for p in "AB":
        got_text(p, 1, 3)
        got_text(p, 3, 1)
    got_images(2, 6)
    columns_of_images(384, 640)
    score_tile(384, 256, 768)
    pass_images(3, 0)
    for p in "AB":
        got_text(p, 1, 2)
        got_text(p, 3, 2)
        send_text(p, (3, 2), (2, 2), second_axis, "-")
    lines_of_text(1, 3)
    score_tile(384, 640, 256)
    pass_images(3, 1)
    score_tile(384, 640, 512)
    got_images(3, 5)
    columns_of_images(128, 384)
    score_tile(128, 256, 768)
    for low, high in pieces:
        image_piece(4, low, high)
        across(4, low, high)
    image_ids(4)
    across_ids(4)
    score_tile(128, 256, 256)
    score_tile(128, 256, 512)
    for p in "AB":
        for e in range(4):
            got_text(p, 2, e)
    lines_of_text(2)
    score_tile(128, 896, 0)
    got_images(4)
    columns_of_images(0, 128)
    for t in range(0, ROWS, 256):
        score_tile(0, 128, t)

    def img_terms(row, count):
        img_part[row:row + count, :] = jnp.dot(coef[row:row + count, :], txts[...], preferred_element_type=f32)

    def txt_terms(row, count):
        txt_part[row:row + count, :] = lax.dot_general(
            coef[:, row:row + count], imgs[...], (((0,), (0,)), ((), ())), preferred_element_type=f32
        )

    def to_core(*blocks):
        for dz in blocks:
            row, rows = IMG_ROW[dz, 1], slice(OWN * dz, OWN * dz + OWN)
            core_send[rows, :] = img_part[row:row + OWN, :].astype(bf16)
            send(("s", dz), core_send.at[rows], core_recv.at[rows], "core")

    def chip_sum(dz, low, high):
        row = IMG_ROW[dz, 0]
        return img_part[row + low:row + high, :] + core_recv[OWN * dz + low:OWN * dz + high, :].astype(f32)

    def z_far():
        hop["s", 4].wait_recv()
        for low, high in pieces:
            z_out(4, low, high, False, "-" if low < HALF else "+")

    def z_out(dz, low, high, before, way):
        rows = slice(OWN * dz + low, OWN * dz + high)
        total = chip_sum(dz, low, high)
        if before:
            hop["r", before, low].wait_recv()
            total = total + z_recv[OWN * before + low:OWN * before + high, :].astype(f32)
        z_send[rows, :] = total.astype(bf16)
        send(("r", dz, low), z_send.at[rows], z_recv.at[rows], "z" + way)

    def z_step(k, which):
        down, up = 4 - k, 4 + k
        for index in range(len(pieces) // 2):
            for dz, before, way, side in ((down, down + 1, "-", 1 - which), (up, up - 1, "+", which)):
                low, high = pieces[side * len(pieces) // 2 + index]
                z_out(dz, low, high, 0 if k == 1 and which == 0 else before, way)

    def txt_far():
        for e in (1, 2, 0, 3):
            for p in "AB":
                base, at = txt_row(p, 2, e), 128 * "AB".index(p) + HALF * e
                t1_send[at:at + HALF, :] = txt_part[base:base + HALF, :].astype(bf16)
                way = "-" if e < 2 else "+"
                send(("t1", p, e), t1_send.at[at:at + HALF], t1_recv.at[at:at + HALF], second_axis[p] + way)

    def txt_near(p, way, e):
        d = 1 if way == "-" else 3
        base, at = txt_row(p, d, e), 256 * "AB".index(p) + 128 * (d // 2) + HALF * e
        total = txt_part[base:base + HALF, :]
        if (way == "-") == (e < 2):
            got = 128 * "AB".index(p) + HALF * e
            hop["t1", p, e].wait_recv()
            total = total + t1_recv[got:got + HALF, :].astype(f32)
        t2_send[at:at + HALF, :] = total.astype(bf16)
        send(("t2", p, way, e), t2_send.at[at:at + HALF], t2_recv.at[at:at + HALF], second_axis[p] + way)

    def txt_line_sum(p, e):
        base, at = txt_row(p, 0, e), 256 * "AB".index(p) + HALF * e
        hop["t2", p, "-", e].wait_recv()
        hop["t2", p, "+", e].wait_recv()
        return (
            txt_part[base:base + HALF, :]
            + t2_recv[at:at + HALF, :].astype(f32)
            + t2_recv[at + 128:at + 128 + HALF, :].astype(f32)
        )

    def txt_far_first(p):
        at = HALF * "AB".index(p)
        t3_send[at:at + HALF, :] = txt_line_sum(p, 2).astype(bf16)
        for part, way in ((0, "-"), (1, "+")):
            rows = slice(at + QUART * part, at + QUART * part + QUART)
            send(("t3", p, part), t3_send.at[rows], t3_recv.at[rows], first_axis[p] + way)

    def txt_near_first(p, part):
        way, e = ("-", 1) if part == 0 else ("+", 3)
        total = txt_line_sum(p, e)
        at = OWN * "AB".index(p) + HALF * part
        for add in (0, 1):
            rows = slice(at + QUART * (part ^ 1 ^ add), at + QUART * (part ^ 1 ^ add) + QUART)
            piece = total[QUART * (part ^ 1 ^ add):QUART * (part ^ 1 ^ add) + QUART]
            if add:
                hop["t3", p, part].wait_recv()
                got = HALF * "AB".index(p) + QUART * part
                piece = piece + t3_recv[got:got + QUART, :].astype(f32)
            t4_send[rows, :] = piece.astype(bf16)
            send(("t4", p, part, add), t4_send.at[rows], t4_recv.at[rows], first_axis[p] + way)

    def finish(embedding, total):
        unit, inverse = unit_rows(embedding)
        direction = scale[:, 0:1] * total
        return inverse * (direction - unit * jnp.sum(unit * direction, axis=1, keepdims=True))

    img_terms(0, 128)
    to_core(4)
    txt_terms(0, 256)
    txt_far()
    img_terms(128, 256)
    to_core(3, 5)
    z_far()
    txt_terms(256, 256)
    txt_near("A", "-", 2)
    txt_near("A", "+", 1)
    txt_near("A", "-", 3)
    txt_terms(512, 256)
    txt_near("B", "-", 2)
    txt_near("B", "+", 1)
    txt_near("B", "-", 3)
    hop["s", 3].wait_recv()
    hop["s", 5].wait_recv()
    z_step(1, 0)
    img_terms(384, 256)
    to_core(2, 6)
    for p in "AB":
        txt_near(p, "+", 2)
        txt_near(p, "-", 1)
    z_step(1, 1)
    img_terms(640, 384)
    to_core(1, 7, 0)
    hop["s", 2].wait_recv()
    hop["s", 6].wait_recv()
    z_step(2, 0)
    for p in "AB":
        txt_near(p, "+", 3)
        txt_near(p, "-", 0)
        txt_near(p, "+", 0)
    txt_terms(768, 256)
    z_step(2, 1)
    txt_far_first("A")
    txt_far_first("B")
    hop["s", 1].wait_recv()
    hop["s", 7].wait_recv()
    z_step(3, 0)
    for p in "AB":
        for part in (0, 1):
            txt_near_first(p, part)
    z_step(3, 1)
    for p in "AB":
        low = HALF * "AB".index(p)
        total = txt_line_sum(p, 0)
        for part in (0, 1):
            for add in (0, 1):
                hop["t4", p, part, add].wait_recv()
            at = OWN * "AB".index(p) + HALF * part
            total = total + t4_recv[at:at + HALF, :].astype(f32)
        txt_out[low:low + HALF, :] = finish(txt_ref[low:low + HALF, :], total)
    hop["s", 0].wait_recv()
    for side in (1, 0):
        low, high = HALF * side, HALF * side + HALF
        total = chip_sum(0, low, high)
        for dz in (1, 7):
            for a, b in pieces:
                if low <= a and b <= high:
                    hop["r", dz, a].wait_recv()
            total = total + z_recv[OWN * dz + low:OWN * dz + high, :].astype(f32)
        img_out[low:high, :] = finish(img_ref[low:high, :], total)
    for copy in started:
        copy.wait_send()


def body(img_emb, txt_emb, img_ids, txt_ids, scale_logarithm, bias):
    f32, bf16, i32 = jnp.float32, jnp.bfloat16, jnp.int32
    vmem, smem = pl.BlockSpec(memory_space=pltpu.VMEM), pl.BlockSpec(memory_space=pltpu.SMEM)
    return pl.pallas_call(
        kernel,
        out_shape=(jax.ShapeDtypeStruct((OWN, D), f32), jax.ShapeDtypeStruct((OWN, D), f32)),
        in_specs=[vmem, vmem, vmem, vmem, smem, smem],
        out_specs=(vmem, vmem),
        scratch_shapes=[
            pltpu.VMEM((ROWS, D), bf16),
            pltpu.VMEM((ROWS, D), bf16),
            pltpu.VMEM((16, 1, 128), i32),
            pltpu.VMEM((32, 1, 128), i32),
            pltpu.VMEM((ROWS, 128), i32),
            pltpu.VMEM((1, ROWS), i32),
            pltpu.VMEM((ROWS, ROWS), bf16),
            pltpu.VMEM((ROWS, D), f32),
            pltpu.VMEM((ROWS, D), f32),
            pltpu.VMEM((256, D), bf16),
            pltpu.VMEM((256, D), bf16),
            pltpu.VMEM((512, D), bf16),
            pltpu.VMEM((512, D), bf16),
            pltpu.VMEM((64, D), bf16),
            pltpu.VMEM((64, D), bf16),
            pltpu.VMEM((128, D), bf16),
            pltpu.VMEM((128, D), bf16),
            pltpu.VMEM((512, D), bf16),
            pltpu.VMEM((512, D), bf16),
            pltpu.VMEM((512, D), bf16),
            pltpu.VMEM((512, D), bf16),
            pltpu.SemaphoreType.DMA((N_COPIES,)),
            pltpu.SemaphoreType.DMA((N_COPIES,)),
        ],
        compiler_params=pltpu.CompilerParams(
            collective_id=0, has_side_effects=True, vmem_limit_bytes=56 * 1024 * 1024
        ),
        cost_estimate=pl.CostEstimate(flops=7247757312, bytes_accessed=900000, transcendentals=1048576),
    )(img_emb, txt_emb, img_ids.reshape(1, OWN), txt_ids.reshape(1, OWN), scale_logarithm, bias)


def solution(mesh):
    split = P(("blk", "group"), None)
    ids = P(("blk", "group"))
    return jax.shard_map(
        body,
        mesh=mesh,
        in_specs=(split, split, ids, ids, P(), P()),
        out_specs=(split, split),
        check_vma=False,
    )
```

time: 71.4 us -> 60.9 us (0.85)
  Pallas kernels: 65.2 us -> 56.3 us
  local copies, waits for them, and re-layouts: 3.39 us -> 2.46 us
    pallas_call x1, Pallas kernels: 65.2 us -> 56.3 us  [body(): pl.pallas_call(kernel, out_shape=(jax.ShapeDtypeStruct((OWN, D), f32), ja...]
    unnamed x8 -> x4, local copies, waits for them, and re-layouts: 3.03 us -> 2.46 us
where the time goes in v1:
time: 60.9 us; the launch traced here: 60.7 us
  Pallas kernels  56.3 us (92%)
  local copies, waits for them, and re-layouts  2.46 us (4%)
  between operations  1.94 us (3%)
    pallas_call x1, Pallas kernels, body(): pl.pallas_call(kernel, out_shape=(jax.ShapeDtypeStruct((OWN, D), f32), ja...  56.3 us
    unnamed x4, local copies, waits for them, and re-layouts  2.46 us

profile of v1, /device:TPU:1, one launch (start us, length us, event | category | flops | bytes accessed | tf_op | source)
XLA Modules:
  0.0 60.7 jit_solution(11420413207822603009)
XLA Ops:
  1.9 56.3 %shard_map.77 = (f32[64,1152]{1,0:T(8,128)}, f32[64,1152]{1,0:T(8,128)}) custom-call(bf16[64,1152]{1,0:T(8,128)(2,1)} %img_ref.1, bf16[64,1152]{1,0:T(8,128)(2,1)} %txt_ref.1, s32[1,64]{1,0:T(1,128)} %bitcast.2, s32[1,64]{1,0:T(1,128)} %bitcast.3, f32[1]{0:T(128)S(6)} %copy.10.scale_ref, f32[1]{0:T(128)S(6)} %copy.11.bias_ref), custom_call_target="tpu_custom_call" | custom-call | flops 7247757312 | bytes 900000 | tf_op jit(solution)/shard_map/pallas_call | solution.py:438
  58.3 0.0 copy-start
  58.3 1.7 %copy.12 = f32[64,1152]{1,0:T(8,128)} copy(f32[64,1152]{1,0:T(8,128)} %get-tuple-element.4) | data formatting | bytes 589824
  60.0 0.0 copy-done
  60.0 0.7 %copy.13 = f32[64,1152]{1,0:T(8,128)} copy(f32[64,1152]{1,0:T(8,128)S(1)} %copy-done) | data formatting | bytes 589824
Async XLA Ops:
  58.3 1.8 %copy-start = (f32[64,1152]{1,0:T(8,128)S(1)}, f32[64,1152]{1,0:T(8,128)}, u32[]{:S(2)}) copy-start(f32[64,1152]{1,0:T(8,128)} %get-tuple-element.5) | copy-start | bytes 884740
